TPU v7x, 32 devices: a whole 2x2x4 slice. The times are simulated.
32 devices in a mesh: head: 4 (over x, core), seq: 8 (over z, y).
Axes of the slice: x: 2, y: 2, z: 4, core: 2. Of those that a mesh axis runs over, the one named last changes fastest.
Arguments:
- tokens: bfloat16 [4, 16, 2048], P(None, None, 'seq'), may hold values from -16 to 16
- attn_in_weight: bfloat16 [3, 2048, 2048], P(None, 'seq', 'head'), may hold values from -0.125 to 0.125
- attn_out_weight: bfloat16 [2048, 2048], P('head', 'seq'), may hold values from -0.125 to 0.125
- ffn_in_weight: bfloat16 [2, 2048, 8192], P(None, 'seq', 'head'), may hold values from -0.125 to 0.125
- ffn_out_weight: bfloat16 [8192, 2048], P('head', 'seq'), may hold values from -0.0625 to 0.0625
- cache_keys: bfloat16 [16, 4096, 2048], P(None, 'seq', 'head'), may hold values from -60 to 60
- cache_values: bfloat16 [16, 4096, 2048], P(None, 'seq', 'head'), may hold values from -10 to 10
- lengths: int32 [16], replicated, may hold values from 1 to 4096, as said below
Outputs:
- attn_branch: bfloat16 [4, 16, 2048], P(None, None, 'seq')
- mlp_branch: bfloat16 [4, 16, 2048], P(None, None, 'seq')
Inputs may be any that keep to these rules, and one draw needn't show every extreme that they name: `lengths`: some request has exactly 4096 filled positions.
All inputs are finite; a program needn't handle non-finite values.
Results may differ from a plain program's by a relative error of at most 0.013.
The roundings to bfloat16 on the way count: a program that leaves them out, or rounds other values in their place, can miss the bound.
Values may be sent and summed in bfloat16 or wider, within the bound.
A program may use at most 64 MiB of HBM per device.

v0:
```python
import jax
import jax.numpy as jnp
from jax import lax
from jax.sharding import PartitionSpec as P

D = 2048
HD = 128


NORM_EPSILON = 1e-05
NEG_FILL = -1e30


def norm_rows(values):
    center = lax.psum(jnp.sum(values, axis=-1), "seq") / D
    deviate = values - center[:, None]
    spread = lax.psum(jnp.sum(deviate * deviate, axis=-1), "seq") / D
    return deviate * lax.rsqrt(spread + NORM_EPSILON)[:, None]


def rotate_pairs(values, positions):
    half_dim = values.shape[-1] // 2
    inverse_freq = 10000.0 ** (-2.0 * jnp.arange(half_dim, dtype=jnp.float32) / values.shape[-1])
    angles = positions.astype(jnp.float32)[:, None, None] * inverse_freq[None, None, :]
    cosine = jnp.cos(angles)
    sine = jnp.sin(angles)
    first_half = values[..., :half_dim]
    second_half = values[..., half_dim:]
    return jnp.concatenate(
        [first_half * cosine - second_half * sine, second_half * cosine + first_half * sine],
        axis=-1,
    )


def combine_parts(earlier, later_part):
    top_one, total_one, acc_one = earlier
    top_two, total_two, acc_two = later_part
    overall = jnp.maximum(top_one, top_two)
    factor_one = jnp.exp(top_one - overall)
    factor_two = jnp.exp(top_two - overall)
    return (
        overall,
        factor_one * total_one + factor_two * total_two,
        factor_one[..., None] * acc_one + factor_two[..., None] * acc_two,
    )


def per_device(
    tokens,
    attn_in_weight,
    attn_out_weight,
    ffn_in_weight,
    ffn_out_weight,
    cache_keys,
    cache_values,
    lengths,
):
    step_count, request_count, width_local = tokens.shape
    row_count = step_count * request_count
    inputs = tokens.reshape(row_count, width_local).astype(jnp.float32)
    normed = norm_rows(inputs).astype(jnp.bfloat16)
    partial_qkv = jnp.einsum(
        "nd,kde->kne", normed, attn_in_weight, preferred_element_type=jnp.float32
    )
    projected = lax.psum(partial_qkv, "seq")
    heads_local = attn_in_weight.shape[2] // HD
    positions = (lengths[None, :] + jnp.arange(step_count, dtype=jnp.int32)[:, None]).reshape(
        row_count
    )
    query = rotate_pairs(projected[0].reshape(row_count, heads_local, HD), positions).astype(
        jnp.bfloat16
    )
    new_keys = rotate_pairs(projected[1].reshape(row_count, heads_local, HD), positions).astype(
        jnp.bfloat16
    )
    new_values = projected[2].reshape(row_count, heads_local, HD).astype(jnp.bfloat16)
    query = query.reshape(step_count, request_count, heads_local, HD)
    new_keys = new_keys.reshape(step_count, request_count, heads_local, HD)
    new_values = new_values.reshape(step_count, request_count, heads_local, HD)
    score_scale = 1.0 / HD**0.5
    block_len = cache_keys.shape[1]
    key_block = cache_keys.reshape(request_count, block_len, heads_local, HD)
    value_block = cache_values.reshape(request_count, block_len, heads_local, HD)
    first_pos = lax.axis_index("seq") * block_len
    scores = (
        jnp.einsum("trhd,rchd->rthc", query, key_block, preferred_element_type=jnp.float32)
        * score_scale
    )
    places = first_pos + jnp.arange(block_len, dtype=jnp.int32)
    valid = (places[None, :] < lengths[:, None])[:, None, None, :]
    block_top = jnp.max(jnp.where(valid, scores, NEG_FILL), axis=-1)
    weights = jnp.where(valid, jnp.exp(scores - block_top[..., None]), 0.0)
    block_total = jnp.sum(weights, axis=-1)
    block_acc = jnp.einsum(
        "rthc,rchd->rthd",
        weights.astype(jnp.bfloat16),
        value_block,
        preferred_element_type=jnp.float32,
    )
    cache_top = lax.pmax(block_top, "seq")
    rescale = jnp.exp(block_top - cache_top)
    cache_total, cache_acc = lax.psum(
        (rescale * block_total, rescale[..., None] * block_acc), "seq"
    )
    new_scores = (
        jnp.einsum("trhd,urhd->rthu", query, new_keys, preferred_element_type=jnp.float32)
        * score_scale
    )
    causal = (jnp.arange(step_count)[:, None] >= jnp.arange(step_count)[None, :])[None, :, None, :]
    new_top = jnp.max(jnp.where(causal, new_scores, NEG_FILL), axis=-1)
    new_weights = jnp.where(causal, jnp.exp(new_scores - new_top[..., None]), 0.0)
    new_total = jnp.sum(new_weights, axis=-1)
    new_acc = jnp.einsum(
        "rthu,urhd->rthd",
        new_weights.astype(jnp.bfloat16),
        new_values,
        preferred_element_type=jnp.float32,
    )
    overall, denom, numer = combine_parts(
        (cache_top, cache_total, cache_acc), (new_top, new_total, new_acc)
    )
    attended = (
        (numer / denom[..., None])
        .transpose(1, 0, 2, 3)
        .reshape(row_count, heads_local * HD)
        .astype(jnp.bfloat16)
    )
    branch = lax.psum(
        jnp.dot(attended, attn_out_weight, preferred_element_type=jnp.float32), "head"
    )
    resid = inputs + branch
    normed_two = norm_rows(resid).astype(jnp.bfloat16)
    both = lax.psum(
        jnp.einsum("nd,kdf->knf", normed_two, ffn_in_weight, preferred_element_type=jnp.float32),
        "seq",
    )
    hidden = (jax.nn.silu(both[0]) * both[1]).astype(jnp.bfloat16)
    mlp_out = lax.psum(jnp.dot(hidden, ffn_out_weight, preferred_element_type=jnp.float32), "head")
    attn_branch = branch.astype(jnp.bfloat16).reshape(step_count, request_count, width_local)
    mlp_branch = mlp_out.astype(jnp.bfloat16).reshape(step_count, request_count, width_local)
    return (attn_branch, mlp_branch)


def solution(mesh):
    in_specs = (
        P(None, None, "seq"),
        P(None, "seq", "head"),
        P("head", "seq"),
        P(None, "seq", "head"),
        P("head", "seq"),
        P(None, "seq", "head"),
        P(None, "seq", "head"),
        P(),
    )
    out_specs = (P(None, None, "seq"), P(None, None, "seq"))
    return jax.shard_map(
        per_device, mesh=mesh, in_specs=in_specs, out_specs=out_specs, check_vma=False
    )
```

profile of v0, /device:TPU:0, one launch (start us, length us, event | category | flops | bytes accessed | tf_op | source)
XLA Modules:
  0.0 444.5 jit_solution(16197547769284160479)
XLA Ops:
  7.2 1.0 convert_reduce_fusion
  8.3 23.1 %psum.70 = f32[64]{0:T(128)S(1)} all-reduce(f32[64]{0:T(128)S(1)} %reduce_sum.59), channel_id=1, replica_groups=mesh['head'=4,'seq'=8] {'seq'}, use_global_device_ids=true, to_apply=%region_1.0 | all-reduce | flops 64 | bytes 512 | tf_op jit(solution)/shard_map/psum | solution.py:15
  31.5 0.9 fusion.41
  32.5 17.1 %psum.71 = f32[64]{0:T(128)S(1)} all-reduce(f32[64]{0:T(128)S(1)} %reduce_sum.61), channel_id=1, replica_groups=mesh['head'=4,'seq'=8] {'seq'}, use_global_device_ids=true, to_apply=%region_3.0 | all-reduce | flops 64 | bytes 512 | tf_op jit(solution)/shard_map/psum | solution.py:17
  49.6 0.8 fusion.43
  50.5 2.1 convolution_bitcast_fusion.1
  54.4 68.4 %all-reduce.5.cloned.1.call-done = f32[3,64,512]{2,1,0:T(8,128)} async-done(((f32[3,64,512]{2,1,0:T(8,128)}), f32[3,64,512]{2,1,0:T(8,128)}) %all-reduce.5.cloned.1.call-update) | async-done | bytes 393232 | tf_op jit(solution)/shard_map/psum | solution.py:65
  122.8 1.0 fusion.64
  125.1 0.9 slice.57
  126.4 5.8 %select_reduce_fusion = (f32[16,4,4]{1,2,0:T(4,128)S(1)}, f32[16,4,4,512]{3,1,2,0:T(4,128)S(1)}) fusion(pred[16,512]{1,0:T(8,128)(4,1)S(1)} %broadcast_compare_fusion, bf16[4,16,4,64]{3,0,2,1:T(4,128)(2,1)S(1)} %copy.64, bf16[4,16,4,64]{3,0,2,1:T(4,128)(2,1)S(1)} %copy.63, bf16[16,512,512]{2,1,0:T(8,128)(2,1)} %param.13), kind=kOutput, calls=%fused_computation.23 | convolution fusion | flops 34078464 | bytes 8987648 | tf_op jit(solution)/shard_map/trhd,rchd->rthc/dot_general | solution.py:86
  132.2 35.3 %pmax.7 = f32[16,4,4]{1,2,0:T(4,128)S(1)} all-reduce(f32[16,4,4]{1,2,0:T(4,128)S(1)} %get-tuple-element.26), channel_id=1, replica_groups=mesh['head'=4,'seq'=8] {'seq'}, use_global_device_ids=true, to_apply=%region_6.7 | all-reduce | flops 256 | bytes 2048 | tf_op jit(solution)/shard_map/pmax | solution.py:100
  167.9 33.0 %psum.74 = f32[16,4,4]{1,2,0:T(4,128)S(1)} all-reduce(f32[16,4,4]{1,2,0:T(4,128)S(1)} %bitcast.130), channel_id=1, replica_groups=mesh['head'=4,'seq'=8] {'seq'}, use_global_device_ids=true, to_apply=%region_10.11 | all-reduce | flops 256 | bytes 2048 | tf_op jit(solution)/shard_map/psum | solution.py:102
  201.0 5.3 %fusion.18 = f32[16,4,4,128]{3,1,2,0:T(4,128)} fusion(f32[16,4,4,512]{3,1,2,0:T(4,128)S(1)} %get-tuple-element.27, f32[16,4,4]{1,2,0:T(4,128)S(1)} %get-tuple-element.26, pred[16,512]{1,0:T(8,128)(4,1)S(1)} %broadcast_compare_fusion, f32[16,4,4]{1,2,0:T(4,128)S(1)} %bitcast.135, bf16[16,512,512]{2,1,0:T(8,128)(2,1)} %param.14), kind=kOutput, calls=%fused_computation.15 | convolution fusion | flops 33980416 | bytes 9054208 | tf_op jit(solution)/shard_map/rthc,rchd->rthd/dot_general | solution.py:94
  206.4 67.0 %all-reduce.7.cloned.1.call-done = f32[16,4,4,128]{3,1,2,0:T(4,128)} async-done(((f32[16,4,4,128]{3,1,2,0:T(4,128)}), f32[16,4,4,128]{3,1,2,0:T(4,128)}) %all-reduce.7.cloned.1.call-update) | async-done | bytes 131088 | tf_op jit(solution)/shard_map/psum | solution.py:102
  273.4 1.2 fusion.22
  275.5 30.6 %all-reduce.9.cloned.1.call-done = f32[64,256]{1,0:T(8,128)} async-done(((f32[64,256]{1,0:T(8,128)}), f32[64,256]{1,0:T(8,128)}) %all-reduce.9.cloned.1.call-update) | async-done | bytes 65552 | tf_op jit(solution)/shard_map/psum | solution.py:128
  306.1 0.9 fusion.55
  307.0 21.4 %psum.76 = f32[64]{0:T(128)S(1)} all-reduce(f32[64]{0:T(128)S(1)} %fusion.55), channel_id=1, replica_groups=mesh['head'=4,'seq'=8] {'seq'}, use_global_device_ids=true, to_apply=%region_14.15 | all-reduce | flops 64 | bytes 512 | tf_op jit(solution)/shard_map/psum | solution.py:15
  328.4 1.6 multiply_reduce_fusion
  330.0 17.1 %psum.77 = f32[64]{0:T(128)S(1)} all-reduce(f32[64]{0:T(128)S(1)} %get-tuple-element.17), channel_id=1, replica_groups=mesh['head'=4,'seq'=8] {'seq'}, use_global_device_ids=true, to_apply=%region_16.17 | all-reduce | flops 64 | bytes 512 | tf_op jit(solution)/shard_map/psum | solution.py:17
  347.2 1.6 convolution_bitcast_fusion
  348.8 75.9 %all-reduce.11.cloned.1.call-done = f32[2,64,2048]{2,1,0:T(8,128)} async-done(((f32[2,64,2048]{2,1,0:T(8,128)}), f32[2,64,2048]{2,1,0:T(8,128)}) %all-reduce.11.cloned.1.call-update) | async-done | bytes 1048592 | tf_op jit(solution)/shard_map/psum | solution.py:133
  424.7 1.9 fusion.30
  426.6 11.4 %psum.79 = bf16[64,256]{1,0:T(8,128)(2,1)} all-reduce(f32[64,256]{1,0:T(8,128)S(1)} %fusion.30), channel_id=1, replica_groups=mesh['head'=4,'seq'=8] {'head'}, use_global_device_ids=true, to_apply=%region_18.19 | all-reduce | flops 16384 | bytes 98304 | tf_op jit(solution)/shard_map/psum | solution.py:138
  (49 shorter events, 5.1 us)
Async XLA Ops:
  7.2 340.0 %copy-start = (bf16[2,256,2048]{2,1,0:T(8,128)(2,1)S(1)}, bf16[2,256,2048]{2,1,0:T(8,128)(2,1)}, u32[]{:S(2)}) copy-start(bf16[2,256,2048]{2,1,0:T(8,128)(2,1)} %param.11) | copy-start | bytes 6291460
  7.2 115.6 %all-reduce.5.cloned.1.call-start = ((), (), s32[]{:S(2)}) async-start(), calls=%async_computation | async-start | bytes 786432 | tf_op jit(solution)/shard_map/psum | solution.py:65
  52.6 220.7 %all-reduce.7.cloned.1.call-start = ((), (), s32[]{:S(2)}) async-start(), calls=%async_computation.1 | async-start | bytes 262144 | tf_op jit(solution)/shard_map/psum | solution.py:102
  132.1 142.5 %copy-start.2 = (bf16[512,256]{1,0:T(8,128)(2,1)S(1)}, bf16[512,256]{1,0:T(8,128)(2,1)}, u32[]{:S(2)}) copy-start(bf16[512,256]{1,0:T(8,128)(2,1)} %param.10) | copy-start | bytes 786436
  132.2 173.9 %copy-start.1 = (bf16[4,16,256]{2,1,0:T(8,128)(2,1)S(1)}, bf16[4,16,256]{2,1,0:T(8,128)(2,1)}, u32[]{:S(2)}) copy-start(bf16[4,16,256]{2,1,0:T(8,128)(2,1)} %param.8) | copy-start | bytes 98308
  206.3 99.7 %all-reduce.9.cloned.1.call-start = ((), (), s32[]{:S(2)}) async-start(), calls=%async_computation.2 | async-start | bytes 131072 | tf_op jit(solution)/shard_map/psum | solution.py:128
  275.4 149.3 %all-reduce.11.cloned.1.call-start = ((), (), s32[]{:S(2)}) async-start(), calls=%async_computation.3 | async-start | bytes 2097152 | tf_op jit(solution)/shard_map/psum | solution.py:133
Sparse Core Ops, SparseCore 0:
  52.8 69.9 all-reduce.4
  206.4 66.8 all-reduce.6
  275.7 30.3 all-reduce.8
  348.9 75.7 all-reduce.10
where the time goes:
time: 445 us; the launch traced here: 444 us
  waiting for transfers between devices  242 us (54%)
  blocking collectives  158 us (36%)
  matrix products  18.9 us (4%)
  between operations  14 us (3%)
  other arithmetic  7.73 us (2%)
    psum x1, waiting for transfers between devices, per_device(): lax.psum(jnp.einsum('nd,kdf->knf', normed_two, ffn_in_weight, preferred_e...  75.9 us
    psum x1, waiting for transfers between devices, per_device(): projected = lax.psum(partial_qkv, 'seq')  68.4 us
    psum x1, waiting for transfers between devices, per_device(): lax.psum((rescale * block_total, rescale[..., None] * block_acc), 'seq')  67 us
    psum x2, blocking collectives, norm_rows(): center = lax.psum(jnp.sum(values, axis=-1), 'seq') / D  44.5 us
    pmax x1, blocking collectives, per_device(): cache_top = lax.pmax(block_top, 'seq')  35.3 us
    psum x2, blocking collectives, norm_rows(): spread = lax.psum(jnp.sum(deviate * deviate, axis=-1), 'seq') / D  34.3 us
    psum x1, blocking collectives, per_device(): lax.psum((rescale * block_total, rescale[..., None] * block_acc), 'seq')  33 us
    psum x1, waiting for transfers between devices, per_device(): lax.psum(jnp.dot(attended, attn_out_weight, preferred_element_type=jnp.fl...  30.6 us
  transfers between devices with their start and end apart: 4, of which 4 were waited for; matrix products, arithmetic and copies ran while one was open for 0% of the time, Pallas kernels for 0%

commit v1 on v0

--- a/solution.py
+++ b/solution.py
@@ -1,10 +1,16 @@
+import functools
+
 import jax
 import jax.numpy as jnp
+import numpy as np
 from jax import lax
+from jax.experimental import pallas as pl
+from jax.experimental.pallas import tpu as pltpu
 from jax.sharding import PartitionSpec as P
 
 D = 2048
 HD = 128
+REQUESTS = 16
 
 
 NORM_EPSILON = 1e-05
@@ -141,6 +147,456 @@
     return (attn_branch, mlp_branch)
 
 
+MESH = pl.DeviceIdType.MESH
+STATS, QKV, QUERY, CACHE, ATTENDED, BRANCH, STATS_TWO, GATE_UP, HIDDEN, DOWN = range(10)
+PHASES = 10
+
+
+def to_row(column, eye):
+    return jnp.sum(jnp.where(eye, column, 0.0), axis=0, keepdims=True)
+
+
+def to_column(row, eye):
+    return jnp.sum(jnp.where(eye, row, 0.0), axis=1, keepdims=True)
+
+
+def layer_kernel(
+    seq_count,
+    head_count,
+    lengths_ref,
+    tokens_ref,
+    freq_ref,
+    win_hbm,
+    wout_hbm,
+    wffn_hbm,
+    wdown_hbm,
+    keys_hbm,
+    values_hbm,
+    attn_out_ref,
+    mlp_out_ref,
+    win,
+    wout,
+    wffn,
+    wdown,
+    keys,
+    values,
+    stats_buf,
+    stats_two_buf,
+    qkv_src,
+    qkv_buf,
+    query_buf,
+    cache_src,
+    cache_buf,
+    attended_buf,
+    branch_buf,
+    gate_src,
+    gate_buf,
+    hidden_buf,
+    down_buf,
+    load_sem,
+    keys_sem,
+    values_sem,
+    send_sem,
+    recv_sem,
+):
+    me = lax.axis_index("seq")
+    head_me = lax.axis_index("head")
+    peers = [lax.rem(me + step, seq_count) for step in range(seq_count)]
+    head_peers = [lax.rem(head_me + step, head_count) for step in range(head_count)]
+    steps, requests, width = tokens_ref.shape
+    rows = steps * requests
+    block_len = keys.shape[1]
+    cols = keys.shape[2]
+    heads = cols // HD
+    total_width = width * seq_count
+
+    weight_loads = [
+        pltpu.make_async_copy(source, target, load_sem.at[index])
+        for index, (source, target) in enumerate(
+            [(win_hbm, win), (wout_hbm, wout), (wffn_hbm, wffn), (wdown_hbm, wdown)]
+        )
+    ]
+
+    def cache_load(hbm, vmem, sem, index):
+        part = pl.ds(2 * index, 2)
+        return pltpu.make_async_copy(hbm.at[part], vmem.at[part], sem.at[index])
+
+    weight_loads[0].start()
+    for peer in peers:
+        cache_load(keys_hbm, keys, keys_sem, peer).start()
+        cache_load(values_hbm, values, values_sem, peer).start()
+    for load in weight_loads[1:]:
+        load.start()
+
+    barrier = pltpu.get_barrier_semaphore()
+    for peer in peers[1:]:
+        pl.semaphore_signal(barrier, inc=1, device_id={"seq": peer}, device_id_type=MESH)
+    for peer in head_peers[1:]:
+        pl.semaphore_signal(barrier, inc=1, device_id={"head": peer}, device_id_type=MESH)
+    pl.semaphore_wait(barrier, seq_count + head_count - 2)
+
+    sent = []
+
+    def send(phase, step, source, target_buf):
+        copy = pltpu.make_async_remote_copy(
+            src_ref=source,
+            dst_ref=target_buf.at[me],
+            send_sem=send_sem.at[phase, step],
+            recv_sem=recv_sem.at[phase, me],
+            device_id={"seq": peers[step]},
+            device_id_type=MESH,
+        )
+        copy.start()
+        sent.append(copy)
+
+    def arrive(phase, step, buf):
+        source = lax.rem(me + seq_count - step, seq_count)
+        pltpu.make_async_remote_copy(
+            src_ref=buf.at[source],
+            dst_ref=buf.at[source],
+            send_sem=send_sem.at[phase, step],
+            recv_sem=recv_sem.at[phase, source],
+            device_id={"seq": peers[step]},
+            device_id_type=MESH,
+        ).wait_recv()
+        return source
+
+    def sum_over_heads(phase, buf, partial):
+        buf[0] = partial.astype(jnp.bfloat16)
+        copies = []
+        for step in range(1, head_count):
+            copy = pltpu.make_async_remote_copy(
+                src_ref=buf.at[0],
+                dst_ref=buf.at[step],
+                send_sem=send_sem.at[phase, step],
+                recv_sem=recv_sem.at[phase, step],
+                device_id={"head": head_peers[step]},
+                device_id_type=MESH,
+            )
+            copy.start()
+            copies.append(copy)
+        sent.extend(copies)
+        for copy in copies:
+            copy.wait_recv()
+        total = jnp.zeros(partial.shape, jnp.float32)
+        for device in range(head_count):
+            slot = lax.rem(head_me + head_count - device, head_count)
+            total = total + buf[slot].astype(jnp.float32)
+        return total
+
+    row_iota = lax.broadcasted_iota(jnp.int32, (rows, 128), 0)
+    lane_iota = lax.broadcasted_iota(jnp.int32, (rows, 128), 1)
+    eye = row_iota == lane_iota
+    sub8 = lax.broadcasted_iota(jnp.int32, (8, 128), 0)
+    lane8 = lax.broadcasted_iota(jnp.int32, (8, 128), 1)
+
+    def normalize(values_in, phase, buf):
+        center = jnp.mean(values_in, axis=1, keepdims=True)
+        deviate = values_in - center
+        spread = jnp.sum(deviate * deviate, axis=1, keepdims=True)
+        buf[me] = jnp.where(
+            sub8 == 0, to_row(center, eye), jnp.where(sub8 == 1, to_row(spread, eye), 0.0)
+        )
+        for step in range(1, seq_count):
+            send(phase, step, buf.at[me], buf)
+        for step in range(1, seq_count):
+            arrive(phase, step, buf)
+        slots = [buf[index] for index in range(seq_count)]
+        mean = sum(slot[0:1] for slot in slots) / seq_count
+        square = sum(
+            slot[1:2] + width * ((slot[0:1] - mean) * (slot[0:1] - mean)) for slot in slots
+        )
+        scale = lax.rsqrt(square / total_width + NORM_EPSILON)
+        return ((values_in - to_column(mean, eye)) * to_column(scale, eye)).astype(jnp.bfloat16)
+
+    perm_row = lax.broadcasted_iota(jnp.int32, (rows, rows), 0)
+    perm_col = lax.broadcasted_iota(jnp.int32, (rows, rows), 1)
+    to_request_major = (
+        (perm_row % steps) * requests + perm_row // steps == perm_col
+    ).astype(jnp.bfloat16)
+    to_step_major = (
+        (perm_col % steps) * requests + perm_col // steps == perm_row
+    ).astype(jnp.bfloat16)
+    inputs = jnp.dot(
+        to_request_major,
+        tokens_ref[...].reshape(rows, width),
+        preferred_element_type=jnp.float32,
+    )
+    normed = normalize(inputs, STATS, stats_buf)
+
+    weight_loads[0].wait()
+    parts = [
+        jnp.dot(normed, win[index], preferred_element_type=jnp.float32) for index in range(3)
+    ]
+    joined = jnp.concatenate(parts, axis=1)
+    half = joined.shape[1] // 2
+    for index in range(seq_count):
+        piece = joined[8 * index : 8 * index + 8]
+        qkv_src[index] = jnp.concatenate([piece[:, :half], piece[:, half:]], axis=0).astype(
+            jnp.bfloat16
+        )
+    for step in range(1, seq_count):
+        send(QKV, step, qkv_src.at[peers[step]], qkv_buf)
+    qkv_buf[me] = qkv_src[me]
+
+    request_of = sub8 // steps
+    length_rows = jnp.where(request_of == 0, lengths_ref[2 * me], lengths_ref[2 * me + 1])
+    position = (length_rows + sub8 % steps).astype(jnp.float32)
+    angles = position * freq_ref[...]
+    cosine = jnp.cos(angles)
+    sine = jnp.sin(angles)
+    sine = jnp.where(lane8 < HD // 2, -sine, sine)
+
+    for step in range(1, seq_count):
+        arrive(QKV, step, qkv_buf)
+    summed = sum(qkv_buf[index].astype(jnp.float32) for index in range(seq_count))
+    projected = jnp.concatenate([summed[:8], summed[8:]], axis=1)
+
+    def rotate(block):
+        out = []
+        for head in range(heads):
+            piece = block[:, head * HD : (head + 1) * HD]
+            out.append(piece * cosine + pltpu.roll(piece, HD // 2, 1) * sine)
+        return jnp.concatenate(out, axis=1)
+
+    query = rotate(projected[:, :cols])
+    query_buf[me] = jnp.concatenate(
+        [query[:, : cols // 2], query[:, cols // 2 :]], axis=0
+    ).astype(jnp.bfloat16)
+    for step in range(1, seq_count):
+        send(QUERY, step, query_buf.at[me], query_buf)
+    new_key = rotate(projected[:, cols : 2 * cols])
+    new_value = projected[:, 2 * cols :]
+
+    score_scale = 1.0 / HD**0.5
+    lane_head = lax.broadcasted_iota(jnp.int32, (8, cols), 1) // HD
+    wide_row = lax.broadcasted_iota(jnp.int32, (8 * heads, block_len), 0) % 8
+    wide_place = lax.broadcasted_iota(jnp.int32, (8 * heads, block_len), 1)
+    acc_row = lax.broadcasted_iota(jnp.int32, (8 * heads, cols), 0) % 8
+
+    def spread_heads(block):
+        return jnp.concatenate(
+            [jnp.where(lane_head == head, block, 0.0) for head in range(heads)], axis=0
+        ).astype(jnp.bfloat16)
+
+    def unpack_query(index):
+        packed = query_buf[index].astype(jnp.float32)
+        return spread_heads(jnp.concatenate([packed[:8], packed[8:]], axis=1))
+
+    def collect(top, total, acc):
+        gathered = jnp.zeros((8, cols), jnp.float32)
+        stats = jnp.zeros((8, 128), jnp.float32)
+        for head in range(heads):
+            piece = slice(8 * head, 8 * head + 8)
+            gathered = jnp.where(lane_head == head, acc[piece], gathered)
+            stats = jnp.where(lane8 == head, top[piece], stats)
+            stats = jnp.where(lane8 == 64 + head, total[piece], stats)
+        return gathered, stats
+
+    contract_last = (((1,), (1,)), ((), ()))
+
+    def cache_block(index):
+        wide_query = unpack_query(index)
+        cache_load(keys_hbm, keys, keys_sem, index).wait()
+        scores = [
+            lax.dot_general(
+                wide_query, keys[2 * index + j], contract_last, preferred_element_type=jnp.float32
+            )
+            for j in range(2)
+        ]
+        scores = jnp.where(wide_row < steps, scores[0], scores[1]) * score_scale
+        limit = jnp.where(
+            wide_row < steps, lengths_ref[2 * index], lengths_ref[2 * index + 1]
+        )
+        valid = wide_place + me * block_len < limit
+        top = jnp.max(jnp.where(valid, scores, NEG_FILL), axis=1, keepdims=True)
+        weights = jnp.where(valid, jnp.exp(scores - top), 0.0)
+        total = jnp.sum(weights, axis=1, keepdims=True)
+        weights = weights.astype(jnp.bfloat16)
+        cache_load(values_hbm, values, values_sem, index).wait()
+        accs = [
+            jnp.dot(weights, values[2 * index + j], preferred_element_type=jnp.float32)
+            for j in range(2)
+        ]
+        return collect(top, total, jnp.where(acc_row < steps, accs[0], accs[1]))
+
+    for step in range(1, seq_count):
+        arrive(QUERY, step, query_buf)
+    for step in list(range(1, seq_count)) + [0]:
+        gathered, stats = cache_block(peers[step])
+        target = cache_src.at[peers[step]] if step else cache_buf.at[me]
+        target[:, :cols] = gathered
+        target[:, cols:] = stats
+        if step:
+            send(CACHE, step, target, cache_buf)
+
+    own_query = unpack_query(me)
+    pad = jnp.zeros((120, cols), jnp.float32)
+    wide_key = jnp.concatenate([new_key, pad], axis=0).astype(jnp.bfloat16)
+    wide_value = jnp.concatenate([new_value, pad], axis=0).astype(jnp.bfloat16)
+    new_scores = (
+        lax.dot_general(own_query, wide_key, contract_last, preferred_element_type=jnp.float32)
+        * score_scale
+    )
+    new_row = lax.broadcasted_iota(jnp.int32, new_scores.shape, 0) % 8
+    new_col = lax.broadcasted_iota(jnp.int32, new_scores.shape, 1)
+    causal = (
+        (new_col < 8)
+        & (new_col // steps == new_row // steps)
+        & (new_col % steps <= new_row % steps)
+    )
+    new_top = jnp.max(jnp.where(causal, new_scores, NEG_FILL), axis=1, keepdims=True)
+    new_weights = jnp.where(causal, jnp.exp(new_scores - new_top), 0.0)
+    new_total = jnp.sum(new_weights, axis=1, keepdims=True)
+    new_acc = jnp.dot(
+        new_weights.astype(jnp.bfloat16), wide_value, preferred_element_type=jnp.float32
+    )
+    blocks = [collect(new_top, new_total, new_acc)]
+
+    for step in range(1, seq_count):
+        arrive(CACHE, step, cache_buf)
+    for index in range(seq_count):
+        blocks.append((cache_buf[index, :, :cols], cache_buf[index, :, cols:]))
+    overall = blocks[0][1]
+    for _, stats in blocks[1:]:
+        overall = jnp.maximum(overall, stats)
+    denom = jnp.zeros((8, 128), jnp.float32)
+    numer = jnp.zeros((8, cols), jnp.float32)
+
+    def over_lanes(block):
+        return jnp.concatenate(
+            [jnp.broadcast_to(block[:, head : head + 1], (8, HD)) for head in range(heads)],
+            axis=1,
+        )
+
+    for acc, stats in blocks:
+        factor = jnp.exp(stats - overall)
+        denom = denom + factor * pltpu.roll(stats, 64, 1)
+        numer = numer + over_lanes(factor) * acc
+    attended = numer / over_lanes(denom)
+    attended_buf[me] = jnp.concatenate(
+        [attended[:, : cols // 2], attended[:, cols // 2 :]], axis=0
+    ).astype(jnp.bfloat16)
+    for step in range(1, seq_count):
+        send(ATTENDED, step, attended_buf.at[me], attended_buf)
+    weight_loads[1].wait()
+    for step in range(1, seq_count):
+        arrive(ATTENDED, step, attended_buf)
+    packed = attended_buf[...].reshape(seq_count * 16, cols // 2)
+    upper = jnp.dot(packed, wout[: cols // 2], preferred_element_type=jnp.float32)
+    lower = jnp.dot(packed, wout[cols // 2 :], preferred_element_type=jnp.float32)
+    partial = (
+        upper.reshape(seq_count, 16, width)[:, :8] + lower.reshape(seq_count, 16, width)[:, 8:]
+    ).reshape(rows, width)
+    branch = sum_over_heads(BRANCH, branch_buf, partial)
+
+    def put_out(ref, value):
+        ref[...] = (
+            jnp.dot(to_step_major, value.astype(jnp.bfloat16), preferred_element_type=jnp.float32)
+            .astype(jnp.bfloat16)
+            .reshape(ref.shape)
+        )
+
+    put_out(attn_out_ref, branch)
+    normed_two = normalize(inputs + branch, STATS_TWO, stats_two_buf)
+
+    weight_loads[2].wait()
+    part = wffn.shape[2] // seq_count
+    for step in list(range(1, seq_count)) + [0]:
+        place = pl.ds(pl.multiple_of(peers[step] * part, part), part)
+        target = gate_src.at[peers[step]] if step else gate_buf.at[me]
+        for index in range(2):
+            target[:, index * part : (index + 1) * part] = jnp.dot(
+                normed_two, wffn[index, :, place], preferred_element_type=jnp.float32
+            ).astype(jnp.bfloat16)
+        if step:
+            send(GATE_UP, step, target, gate_buf)
+    for step in range(1, seq_count):
+        arrive(GATE_UP, step, gate_buf)
+    both = sum(gate_buf[index].astype(jnp.float32) for index in range(seq_count))
+    gate = both[:, :part]
+    hidden_buf[me] = (gate / (1.0 + jnp.exp(-gate)) * both[:, part:]).astype(jnp.bfloat16)
+    for step in range(1, seq_count):
+        send(HIDDEN, step, hidden_buf.at[me], hidden_buf)
+    weight_loads[3].wait()
+    partial = jnp.zeros((rows, width), jnp.float32)
+    for step in range(seq_count):
+        source = arrive(HIDDEN, step, hidden_buf) if step else me
+        place = pl.ds(pl.multiple_of(source * part, part), part)
+        partial = partial + jnp.dot(
+            hidden_buf[source], wdown[place, :], preferred_element_type=jnp.float32
+        )
+    put_out(mlp_out_ref, sum_over_heads(DOWN, down_buf, partial))
+    for copy in sent:
+        copy.wait_send()
+
+
+def fused_device(
+    tokens,
+    attn_in_weight,
+    attn_out_weight,
+    ffn_in_weight,
+    ffn_out_weight,
+    cache_keys,
+    cache_values,
+    lengths,
+    *,
+    seq_count,
+    head_count,
+):
+    rows = tokens.shape[0] * tokens.shape[1]
+    width = tokens.shape[2]
+    cols = cache_keys.shape[2]
+    part = ffn_in_weight.shape[2] // seq_count
+    inverse_freq = 10000.0 ** (-2.0 * np.arange(HD // 2) / HD)
+    freq = jnp.asarray(np.tile(inverse_freq, 2)[None, :].astype(np.float32))
+    bf16, f32 = jnp.bfloat16, jnp.float32
+    in_vmem = pl.BlockSpec(memory_space=pltpu.VMEM)
+    in_any = pl.BlockSpec(memory_space=pl.ANY)
+    weights = (attn_in_weight, attn_out_weight, ffn_in_weight, ffn_out_weight)
+    caches = (cache_keys, cache_values)
+    return pl.pallas_call(
+        functools.partial(layer_kernel, seq_count, head_count),
+        out_shape=[jax.ShapeDtypeStruct(tokens.shape, bf16)] * 2,
+        in_specs=[pl.BlockSpec(memory_space=pltpu.SMEM), in_vmem, in_vmem] + [in_any] * 6,
+        out_specs=[in_vmem] * 2,
+        scratch_shapes=[pltpu.VMEM(array.shape, bf16) for array in weights + caches]
+        + [
+            pltpu.VMEM((seq_count, 8, 128), f32),
+            pltpu.VMEM((seq_count, 8, 128), f32),
+            pltpu.VMEM((seq_count, 16, 3 * cols // 2), bf16),
+            pltpu.VMEM((seq_count, 16, 3 * cols // 2), bf16),
+            pltpu.VMEM((seq_count, 16, cols // 2), bf16),
+            pltpu.VMEM((seq_count, 8, cols + 128), f32),
+            pltpu.VMEM((seq_count, 8, cols + 128), f32),
+            pltpu.VMEM((seq_count, 16, cols // 2), bf16),
+            pltpu.VMEM((head_count, rows, width), bf16),
+            pltpu.VMEM((seq_count, rows, 2 * part), bf16),
+            pltpu.VMEM((seq_count, rows, 2 * part), bf16),
+            pltpu.VMEM((seq_count, rows, part), bf16),
+            pltpu.VMEM((head_count, rows, width), bf16),
+            pltpu.SemaphoreType.DMA((4,)),
+            pltpu.SemaphoreType.DMA((seq_count,)),
+            pltpu.SemaphoreType.DMA((seq_count,)),
+            pltpu.SemaphoreType.DMA((PHASES, max(seq_count, head_count))),
+            pltpu.SemaphoreType.DMA((PHASES, max(seq_count, head_count))),
+        ],
+        compiler_params=pltpu.CompilerParams(
+            collective_id=0, has_side_effects=True, vmem_limit_bytes=48 * 2**20
+        ),
+        cost_estimate=pl.CostEstimate(
+            flops=2 * rows * width * (attn_in_weight.size + ffn_in_weight.size) // width,
+            bytes_accessed=2 * sum(array.size for array in weights + caches),
+            transcendentals=0,
+        ),
+    )(lengths, tokens, freq, *weights, *caches)
+
+
+def fits_fused(mesh):
+    seq_count, head_count = mesh.shape["seq"], mesh.shape["head"]
+    return REQUESTS == 2 * seq_count and D % (128 * seq_count) == 0 and D % (256 * head_count) == 0
+
+
 def solution(mesh):
     in_specs = (
         P(None, None, "seq"),
@@ -153,6 +609,11 @@
         P(),
     )
     out_specs = (P(None, None, "seq"), P(None, None, "seq"))
+    body = per_device
+    if fits_fused(mesh):
+        body = functools.partial(
+            fused_device, seq_count=mesh.shape["seq"], head_count=mesh.shape["head"]
+        )
     return jax.shard_map(
-        per_device, mesh=mesh, in_specs=in_specs, out_specs=out_specs, check_vma=False
-    )
+        body, mesh=mesh, in_specs=in_specs, out_specs=out_specs, check_vma=False
+    )

time: 445 us -> 76.3 us (0.17)
  waiting for transfers between devices: 242 us -> 0 us
  blocking collectives: 158 us -> 0 us
  Pallas kernels: 0 us -> 67.1 us
  matrix products: 18.9 us -> 0 us
  between operations: 14 us -> 0.66 us
  other arithmetic: 7.73 us -> 0 us
  local copies, waits for them, and re-layouts: 3.32 us -> 8.19 us
    psum x4 -> x0, waiting for transfers between devices: 242 us -> none  [the longest x1 75.9 us: per_device(): lax.psum(jnp.einsum('nd,kdf->knf', normed_two, ffn_in_weight, preferred_e...]
    psum x6 -> x0, blocking collectives: 123 us -> none  [the longest x2 44.5 us: norm_rows(): center = lax.psum(jnp.sum(values, axis=-1), 'seq') / D]
    pallas_call x0 -> x1, Pallas kernels: none -> 67.1 us  [fused_device(): pl.pallas_call(functools.partial(layer_kernel, seq_count, head_count), ou...]
    pmax x1 -> x0, blocking collectives: 35.3 us -> none  [per_device(): cache_top = lax.pmax(block_top, 'seq')]
    dot_general x8 -> x0, matrix products: 18.9 us -> none  [the longest x1 5.77 us: per_device(): jnp.einsum('trhd,rchd->rthc', query, key_block, preferred_element_type=jn...]
    unnamed x6 -> x16, local copies, waits for them, and re-layouts: 0.03 us -> 8.19 us
    reduce_sum x6 -> x0, other arithmetic: 5.03 us -> none  [the longest x2 2.56 us: norm_rows(): spread = lax.psum(jnp.sum(deviate * deviate, axis=-1), 'seq') / D]
  transfers between devices with their start and end apart: 4 -> 0, of which waited for: 4 -> 0; matrix products, arithmetic and copies ran while one was open for 0% -> 0% of each run, Pallas kernels for 0% -> 0%
where the time goes in v1:
time: 76.3 us; the launch traced here: 76 us
  Pallas kernels  67.1 us (88%)
  local copies, waits for them, and re-layouts  8.19 us (11%)
    pallas_call x1, Pallas kernels, fused_device(): pl.pallas_call(functools.partial(layer_kernel, seq_count, head_count), ou...  67.1 us
    unnamed x16, local copies, waits for them, and re-layouts  8.19 us

profile of v1, /device:TPU:0, one launch (start us, length us, event | category | flops | bytes accessed | tf_op | source)
XLA Modules:
  0.0 76.0 jit_solution(11062159705636167053)
XLA Ops:
  0.6 0.0 copy-start
  0.6 1.6 %copy-done = bf16[2,256,2048]{2,1,0:T(8,128)(2,1)S(1)} copy-done((bf16[2,256,2048]{2,1,0:T(8,128)(2,1)S(1)}, bf16[2,256,2048]{2,1,0:T(8,128)(2,1)}, u32[]{:S(2)}) %copy-start) | copy-done | bytes 2097176
  2.2 0.0 copy-start.1
  2.2 1.2 %copy-done.1 = bf16[2048,256]{1,0:T(8,128)(2,1)S(1)} copy-done((bf16[2048,256]{1,0:T(8,128)(2,1)S(1)}, bf16[2048,256]{1,0:T(8,128)(2,1)}, u32[]{:S(2)}) %copy-start.1) | copy-done | bytes 1048600
  3.5 0.0 copy-start.2
  3.5 1.1 %copy-done.2 = bf16[3,256,512]{2,1,0:T(8,128)(2,1)S(1)} copy-done((bf16[3,256,512]{2,1,0:T(8,128)(2,1)S(1)}, bf16[3,256,512]{2,1,0:T(8,128)(2,1)}, u32[]{:S(2)}) %copy-start.2) | copy-done | bytes 786456
  4.6 0.0 copy-start.3
  4.6 0.9 %copy-done.3 = bf16[512,256]{1,0:T(8,128)(2,1)S(1)} copy-done((bf16[512,256]{1,0:T(8,128)(2,1)S(1)}, bf16[512,256]{1,0:T(8,128)(2,1)}, u32[]{:S(2)}) %copy-start.3) | copy-done | bytes 262168
  5.5 0.0 copy-start.4
  5.5 0.8 copy-done.4
  6.3 0.0 copy-start.5
  6.3 0.7 copy-done.5
  6.9 0.0 copy-start.6
  7.0 0.7 copy-done.6
  7.6 67.1 %shard_map.104 = (bf16[4,16,256]{2,1,0:T(8,128)(2,1)S(1)}, bf16[4,16,256]{2,1,0:T(8,128)(2,1)S(1)}) custom-call(s32[16]{0:T(128)S(1)} %copy-done.5, bf16[4,16,256]{2,1,0:T(8,128)(2,1)S(1)} %copy-done.4, f32[1,128]{1,0:T(1,128)S(1)} %copy-done.6, bf16[3,256,512]{2,1,0:T(8,128)(2,1)S(1)} %copy-done.2, bf16[512,256]{1,0:T(8,128)(2,1)S(1)} %copy-done.3, ...), custom_call_target="tpu_custom_call" | custom-call | flops 184549376 | bytes 20971520 | tf_op jit(solution)/shard_map/pallas_call | solution.py:558
  74.8 0.6 copy.13
  75.4 0.6 copy.14
Async XLA Ops:
  0.6 1.6 %copy-start = (bf16[2,256,2048]{2,1,0:T(8,128)(2,1)S(1)}, bf16[2,256,2048]{2,1,0:T(8,128)(2,1)}, u32[]{:S(2)}) copy-start(bf16[2,256,2048]{2,1,0:T(8,128)(2,1)} %wffn_hbm.1) | copy-start | bytes 6291460
  2.2 1.2 %copy-start.1 = (bf16[2048,256]{1,0:T(8,128)(2,1)S(1)}, bf16[2048,256]{1,0:T(8,128)(2,1)}, u32[]{:S(2)}) copy-start(bf16[2048,256]{1,0:T(8,128)(2,1)} %wdown_hbm.1) | copy-start | bytes 3145732
  3.5 1.1 %copy-start.2 = (bf16[3,256,512]{2,1,0:T(8,128)(2,1)S(1)}, bf16[3,256,512]{2,1,0:T(8,128)(2,1)}, u32[]{:S(2)}) copy-start(bf16[3,256,512]{2,1,0:T(8,128)(2,1)} %win_hbm.1) | copy-start | bytes 2359300
  4.6 0.9 %copy-start.3 = (bf16[512,256]{1,0:T(8,128)(2,1)S(1)}, bf16[512,256]{1,0:T(8,128)(2,1)}, u32[]{:S(2)}) copy-start(bf16[512,256]{1,0:T(8,128)(2,1)} %wout_hbm.1) | copy-start | bytes 786436
  5.5 0.8 copy-start.4
  6.3 0.7 copy-start.5
  6.9 0.7 copy-start.6

commit v2 on v1

--- a/solution.py
+++ b/solution.py
@@ -148,8 +148,12 @@
 
 
 MESH = pl.DeviceIdType.MESH
-STATS, QKV, QUERY, CACHE, ATTENDED, BRANCH, STATS_TWO, GATE_UP, HIDDEN, DOWN = range(10)
-PHASES = 10
+(
+    STATS, QKV, QUERY, CACHE, ATTENDED, BRANCH, STATS_TWO, GATE_UP, HIDDEN, DOWN,
+    COLUMN_SUM, GATE_UP_PAIR, HIDDEN_PAIR,
+) = range(13)
+PHASES = 13
+PAIR = 2
 
 
 def to_row(column, eye):
@@ -189,8 +193,12 @@
     cache_buf,
     attended_buf,
     branch_buf,
-    gate_src,
-    gate_buf,
+    column_src,
+    column_buf,
+    pair_src,
+    pair_buf,
+    line_src,
+    line_buf,
     hidden_buf,
     down_buf,
     load_sem,
@@ -236,6 +244,28 @@
     pl.semaphore_wait(barrier, seq_count + head_count - 2)
 
     sent = []
+
+    def push(source, target, send_slot, recv_slot, peer):
+        copy = pltpu.make_async_remote_copy(
+            src_ref=source,
+            dst_ref=target,
+            send_sem=send_sem.at[send_slot[0], send_slot[1]],
+            recv_sem=recv_sem.at[recv_slot[0], recv_slot[1]],
+            device_id={"seq": peer},
+            device_id_type=MESH,
+        )
+        copy.start()
+        sent.append(copy)
+
+    def landed(buf, recv_slot):
+        pltpu.make_async_remote_copy(
+            src_ref=buf,
+            dst_ref=buf,
+            send_sem=send_sem.at[recv_slot[0], 0],
+            recv_sem=recv_sem.at[recv_slot[0], recv_slot[1]],
+            device_id={"seq": peers[1]},
+            device_id_type=MESH,
+        ).wait_recv()
 
     def send(phase, step, source, target_buf):
         copy = pltpu.make_async_remote_copy(
@@ -290,7 +320,7 @@
     sub8 = lax.broadcasted_iota(jnp.int32, (8, 128), 0)
     lane8 = lax.broadcasted_iota(jnp.int32, (8, 128), 1)
 
-    def normalize(values_in, phase, buf):
+    def send_stats(values_in, phase, buf):
         center = jnp.mean(values_in, axis=1, keepdims=True)
         deviate = values_in - center
         spread = jnp.sum(deviate * deviate, axis=1, keepdims=True)
@@ -299,15 +329,18 @@
         )
         for step in range(1, seq_count):
             send(phase, step, buf.at[me], buf)
+        return deviate
+
+    def join_stats(phase, buf):
         for step in range(1, seq_count):
             arrive(phase, step, buf)
         slots = [buf[index] for index in range(seq_count)]
         mean = sum(slot[0:1] for slot in slots) / seq_count
+        offsets = [slot[0:1] - mean for slot in slots]
         square = sum(
-            slot[1:2] + width * ((slot[0:1] - mean) * (slot[0:1] - mean)) for slot in slots
-        )
-        scale = lax.rsqrt(square / total_width + NORM_EPSILON)
-        return ((values_in - to_column(mean, eye)) * to_column(scale, eye)).astype(jnp.bfloat16)
+            slot[1:2] + width * (offset * offset) for slot, offset in zip(slots, offsets)
+        )
+        return mean, offsets, lax.rsqrt(square / total_width + NORM_EPSILON)
 
     perm_row = lax.broadcasted_iota(jnp.int32, (rows, rows), 0)
     perm_col = lax.broadcasted_iota(jnp.int32, (rows, rows), 1)
@@ -322,7 +355,9 @@
         tokens_ref[...].reshape(rows, width),
         preferred_element_type=jnp.float32,
     )
-    normed = normalize(inputs, STATS, stats_buf)
+    send_stats(inputs, STATS, stats_buf)
+    mean, _, scale = join_stats(STATS, stats_buf)
+    normed = ((inputs - to_column(mean, eye)) * to_column(scale, eye)).astype(jnp.bfloat16)
 
     weight_loads[0].wait()
     parts = [
@@ -367,6 +402,25 @@
         send(QUERY, step, query_buf.at[me], query_buf)
     new_key = rotate(projected[:, cols : 2 * cols])
     new_value = projected[:, 2 * cols :]
+
+    part = wffn.shape[2] // seq_count
+    weight_loads[2].wait()
+    ones = jnp.ones((16, width), jnp.bfloat16)
+    column_sums = [
+        jnp.dot(ones, wffn[index], preferred_element_type=jnp.float32)[:8] for index in range(2)
+    ]
+    pieces = part // 128
+    for index in range(seq_count):
+        packed = jnp.zeros((8, 128), jnp.float32)
+        for piece in range(2 * pieces):
+            start = index * part + (piece % pieces) * 128
+            packed = jnp.where(
+                sub8 == piece, column_sums[piece // pieces][:, start : start + 128], packed
+            )
+        column_src[index] = packed
+    column_buf[me] = column_src[me]
+    for step in range(1, seq_count):
+        send(COLUMN_SUM, step, column_src.at[peers[step]], column_buf)
 
     score_scale = 1.0 / HD**0.5
     lane_head = lax.broadcasted_iota(jnp.int32, (8, cols), 1) // HD
@@ -498,34 +552,78 @@
         )
 
     put_out(attn_out_ref, branch)
-    normed_two = normalize(inputs + branch, STATS_TWO, stats_two_buf)
-
-    weight_loads[2].wait()
-    part = wffn.shape[2] // seq_count
-    for step in list(range(1, seq_count)) + [0]:
-        place = pl.ds(pl.multiple_of(peers[step] * part, part), part)
-        target = gate_src.at[peers[step]] if step else gate_buf.at[me]
-        for index in range(2):
-            target[:, index * part : (index + 1) * part] = jnp.dot(
-                normed_two, wffn[index, :, place], preferred_element_type=jnp.float32
-            ).astype(jnp.bfloat16)
+    lines = seq_count // PAIR
+    line, place_in_pair = me // PAIR, me % PAIR
+    partner = line * PAIR + (PAIR - 1 - place_in_pair)
+    line_peers = [lax.rem(line + step, lines) * PAIR + place_in_pair for step in range(lines)]
+    across = [lax.rem(line + step, lines) * PAIR + (PAIR - 1 - place_in_pair) for step in range(lines)]
+    centred = send_stats(inputs + branch, STATS_TWO, stats_two_buf).astype(jnp.bfloat16)
+
+    def gate_up(index):
+        place = pl.ds(pl.multiple_of(index * part, part), part)
+        return jnp.concatenate(
+            [
+                jnp.dot(centred, wffn[which, :, place], preferred_element_type=jnp.float32)
+                for which in range(2)
+            ],
+            axis=1,
+        )
+
+    order = list(range(1, lines)) + [0]
+    for step in order:
+        pair_src[step] = gate_up(across[step]).astype(jnp.bfloat16)
+        push(
+            pair_src.at[step], pair_buf.at[step], (GATE_UP_PAIR, step), (GATE_UP_PAIR, step), partner
+        )
+    for step in order:
+        own = gate_up(line_peers[step])
+        landed(pair_buf.at[step], (GATE_UP_PAIR, step))
+        both = own + pair_buf[step].astype(jnp.float32)
         if step:
-            send(GATE_UP, step, target, gate_buf)
-    for step in range(1, seq_count):
-        arrive(GATE_UP, step, gate_buf)
-    both = sum(gate_buf[index].astype(jnp.float32) for index in range(seq_count))
+            line_src[step] = both.astype(jnp.bfloat16)
+            push(
+                line_src.at[step],
+                line_buf.at[step],
+                (GATE_UP, step),
+                (GATE_UP, step),
+                line_peers[step],
+            )
+    _, offsets, scale = join_stats(STATS_TWO, stats_two_buf)
+    for step in range(1, seq_count):
+        arrive(COLUMN_SUM, step, column_buf)
+    for index in range(seq_count):
+        sums = column_buf[index]
+        sums = jnp.concatenate([sums[j : j + 1] for j in range(2 * pieces)], axis=1)
+        both = both + to_column(offsets[index], eye) * sums
+    scale = to_column(scale, eye)
+    for step in range(1, lines):
+        landed(line_buf.at[step], (GATE_UP, step))
+        both = both + line_buf[step].astype(jnp.float32)
+    both = both * scale
     gate = both[:, :part]
     hidden_buf[me] = (gate / (1.0 + jnp.exp(-gate)) * both[:, part:]).astype(jnp.bfloat16)
-    for step in range(1, seq_count):
-        send(HIDDEN, step, hidden_buf.at[me], hidden_buf)
+
+    def share(index, step):
+        push(
+            hidden_buf.at[index], hidden_buf.at[index], (HIDDEN_PAIR, step), (HIDDEN, index), partner
+        )
+
+    def down(index):
+        place = pl.ds(pl.multiple_of(index * part, part), part)
+        return jnp.dot(hidden_buf[index], wdown[place, :], preferred_element_type=jnp.float32)
+
+    for step in range(1, lines):
+        push(hidden_buf.at[me], hidden_buf.at[me], (HIDDEN, step), (HIDDEN, me), line_peers[step])
+    share(me, 0)
     weight_loads[3].wait()
-    partial = jnp.zeros((rows, width), jnp.float32)
-    for step in range(seq_count):
-        source = arrive(HIDDEN, step, hidden_buf) if step else me
-        place = pl.ds(pl.multiple_of(source * part, part), part)
-        partial = partial + jnp.dot(
-            hidden_buf[source], wdown[place, :], preferred_element_type=jnp.float32
-        )
+    partial = down(me)
+    for step in range(1, lines):
+        landed(hidden_buf.at[line_peers[step]], (HIDDEN, line_peers[step]))
+        share(line_peers[step], step)
+        partial = partial + down(line_peers[step])
+    for step in range(lines):
+        landed(hidden_buf.at[across[step]], (HIDDEN, across[step]))
+        partial = partial + down(across[step])
     put_out(mlp_out_ref, sum_over_heads(DOWN, down_buf, partial))
     for copy in sent:
         copy.wait_send()
@@ -571,8 +669,12 @@
             pltpu.VMEM((seq_count, 8, cols + 128), f32),
             pltpu.VMEM((seq_count, 16, cols // 2), bf16),
             pltpu.VMEM((head_count, rows, width), bf16),
-            pltpu.VMEM((seq_count, rows, 2 * part), bf16),
-            pltpu.VMEM((seq_count, rows, 2 * part), bf16),
+            pltpu.VMEM((seq_count, 8, 128), f32),
+            pltpu.VMEM((seq_count, 8, 128), f32),
+            pltpu.VMEM((seq_count // PAIR, rows, 2 * part), bf16),
+            pltpu.VMEM((seq_count // PAIR, rows, 2 * part), bf16),
+            pltpu.VMEM((seq_count // PAIR, rows, 2 * part), bf16),
+            pltpu.VMEM((seq_count // PAIR, rows, 2 * part), bf16),
             pltpu.VMEM((seq_count, rows, part), bf16),
             pltpu.VMEM((head_count, rows, width), bf16),
             pltpu.SemaphoreType.DMA((4,)),
@@ -582,7 +684,7 @@
             pltpu.SemaphoreType.DMA((PHASES, max(seq_count, head_count))),
         ],
         compiler_params=pltpu.CompilerParams(
-            collective_id=0, has_side_effects=True, vmem_limit_bytes=48 * 2**20
+            collective_id=0, has_side_effects=True, vmem_limit_bytes=60 * 2**20
         ),
         cost_estimate=pl.CostEstimate(
             flops=2 * rows * width * (attn_in_weight.size + ffn_in_weight.size) // width,

time: 76.3 us -> 67.3 us (0.88)
  local copies, waits for them, and re-layouts: 8.19 us -> 2.75 us
  Pallas kernels: 67.1 us -> 63.6 us
    unnamed x16 -> x2, local copies, waits for them, and re-layouts: 8.19 us -> 2.75 us
    pallas_call x1, Pallas kernels: 67.1 us -> 63.6 us  [fused_device(): pl.pallas_call(functools.partial(layer_kernel, seq_count, head_count), ou...]
where the time goes in v2:
time: 67.3 us; the launch traced here: 67 us
  Pallas kernels  63.6 us (95%)
  local copies, waits for them, and re-layouts  2.75 us (4%)
    pallas_call x1, Pallas kernels, fused_device(): pl.pallas_call(functools.partial(layer_kernel, seq_count, head_count), ou...  63.6 us
    unnamed x2, local copies, waits for them, and re-layouts  2.75 us

profile of v2, /device:TPU:0, one launch (start us, length us, event | category | flops | bytes accessed | tf_op | source)
XLA Modules:
  0.0 67.0 jit_solution(13080095545371257902)
XLA Ops:
  0.6 63.6 %shard_map.104 = (bf16[4,16,256]{2,1,0:T(8,128)(2,1)}, bf16[4,16,256]{2,1,0:T(8,128)(2,1)}) custom-call(s32[16]{0:T(128)} %lengths_ref.1, bf16[4,16,256]{2,1,0:T(8,128)(2,1)} %tokens_ref.1, f32[1,128]{1,0:T(1,128)} %constant.2.clone.freq_ref, bf16[3,256,512]{2,1,0:T(8,128)(2,1)} %win_hbm.1, bf16[512,256]{1,0:T(8,128)(2,1)} %wout_hbm.1, ...), custom_call_target="tpu_custom_call" | custom-call | flops 184549376 | bytes 20971520 | tf_op jit(solution)/shard_map/pallas_call | solution.py:656
  64.2 1.4 %copy.13 = bf16[4,16,256]{2,1,0:T(8,128)(2,1)} copy(bf16[4,16,256]{2,1,0:T(8,128)(2,1)} %get-tuple-element.4) | data formatting | bytes 65536
  65.6 1.4 %copy.14 = bf16[4,16,256]{2,1,0:T(8,128)(2,1)} copy(bf16[4,16,256]{2,1,0:T(8,128)(2,1)} %get-tuple-element.5) | data formatting | bytes 65536

commit v3 on v2

--- a/solution.py
+++ b/solution.py
@@ -170,7 +170,7 @@
     lengths_ref,
     tokens_ref,
     freq_ref,
-    win_hbm,
+    win_any,
     wout_hbm,
     wffn_hbm,
     wdown_hbm,
@@ -221,7 +221,7 @@
     weight_loads = [
         pltpu.make_async_copy(source, target, load_sem.at[index])
         for index, (source, target) in enumerate(
-            [(win_hbm, win), (wout_hbm, wout), (wffn_hbm, wffn), (wdown_hbm, wdown)]
+            [(win_any, win), (wout_hbm, wout), (wffn_hbm, wffn), (wdown_hbm, wdown)]
         )
     ]
 
@@ -317,6 +317,9 @@
     row_iota = lax.broadcasted_iota(jnp.int32, (rows, 128), 0)
     lane_iota = lax.broadcasted_iota(jnp.int32, (rows, 128), 1)
     eye = row_iota == lane_iota
+    eye128 = lax.broadcasted_iota(jnp.int32, (128, 128), 0) == lax.broadcasted_iota(
+        jnp.int32, (128, 128), 1
+    )
     sub8 = lax.broadcasted_iota(jnp.int32, (8, 128), 0)
     lane8 = lax.broadcasted_iota(jnp.int32, (8, 128), 1)
 
@@ -424,8 +427,6 @@
 
     score_scale = 1.0 / HD**0.5
     lane_head = lax.broadcasted_iota(jnp.int32, (8, cols), 1) // HD
-    wide_row = lax.broadcasted_iota(jnp.int32, (8 * heads, block_len), 0) % 8
-    wide_place = lax.broadcasted_iota(jnp.int32, (8 * heads, block_len), 1)
     acc_row = lax.broadcasted_iota(jnp.int32, (8 * heads, cols), 0) % 8
 
     def spread_heads(block):
@@ -449,40 +450,60 @@
 
     contract_last = (((1,), (1,)), ((), ()))
 
-    def cache_block(index):
-        wide_query = unpack_query(index)
-        cache_load(keys_hbm, keys, keys_sem, index).wait()
-        scores = [
-            lax.dot_general(
-                wide_query, keys[2 * index + j], contract_last, preferred_element_type=jnp.float32
+    chunk = 8 * heads
+    together = 128 // chunk
+    score_col = lax.broadcasted_iota(jnp.int32, (cols, 128), 1)
+    place_col = lax.broadcasted_iota(jnp.int32, (block_len, 128), 1)
+    places = lax.broadcasted_iota(jnp.int32, (block_len, 128), 0) + me * block_len
+
+    def cache_blocks(indices):
+        wide = jnp.concatenate([unpack_query(index) for index in indices], axis=0)
+        wide = wide.astype(jnp.float32).T
+        scores = jnp.zeros((block_len, 128), jnp.float32)
+        limit = jnp.zeros((block_len, 128), jnp.int32)
+        for spot, index in enumerate(indices):
+            cache_load(keys_hbm, keys, keys_sem, index).wait()
+            for j in range(2):
+                mine = (score_col // chunk == spot) & (score_col % 8 // steps == j)
+                scores = scores + jnp.dot(
+                    keys[2 * index + j],
+                    jnp.where(mine, wide, 0.0).astype(jnp.bfloat16),
+                    preferred_element_type=jnp.float32,
+                )
+                mine = (place_col // chunk == spot) & (place_col % 8 // steps == j)
+                limit = jnp.where(mine, lengths_ref[2 * index + j], limit)
+        scores = scores * score_scale
+        valid = places < limit
+        top = jnp.max(jnp.where(valid, scores, NEG_FILL), axis=0, keepdims=True)
+        weights = jnp.where(valid, jnp.exp(scores - top), 0.0)
+        total = jnp.sum(weights, axis=0, keepdims=True)
+        top = to_column(top, eye128)
+        total = to_column(total, eye128)
+        weights = weights.T.astype(jnp.bfloat16)
+        out = []
+        for spot, index in enumerate(indices):
+            cache_load(values_hbm, values, values_sem, index).wait()
+            here = slice(spot * chunk, (spot + 1) * chunk)
+            accs = [
+                jnp.dot(weights[here], values[2 * index + j], preferred_element_type=jnp.float32)
+                for j in range(2)
+            ]
+            out.append(
+                collect(top[here], total[here], jnp.where(acc_row < steps, accs[0], accs[1]))
             )
-            for j in range(2)
-        ]
-        scores = jnp.where(wide_row < steps, scores[0], scores[1]) * score_scale
-        limit = jnp.where(
-            wide_row < steps, lengths_ref[2 * index], lengths_ref[2 * index + 1]
-        )
-        valid = wide_place + me * block_len < limit
-        top = jnp.max(jnp.where(valid, scores, NEG_FILL), axis=1, keepdims=True)
-        weights = jnp.where(valid, jnp.exp(scores - top), 0.0)
-        total = jnp.sum(weights, axis=1, keepdims=True)
-        weights = weights.astype(jnp.bfloat16)
-        cache_load(values_hbm, values, values_sem, index).wait()
-        accs = [
-            jnp.dot(weights, values[2 * index + j], preferred_element_type=jnp.float32)
-            for j in range(2)
-        ]
-        return collect(top, total, jnp.where(acc_row < steps, accs[0], accs[1]))
+        return out
 
     for step in range(1, seq_count):
         arrive(QUERY, step, query_buf)
-    for step in list(range(1, seq_count)) + [0]:
-        gathered, stats = cache_block(peers[step])
-        target = cache_src.at[peers[step]] if step else cache_buf.at[me]
-        target[:, :cols] = gathered
-        target[:, cols:] = stats
-        if step:
-            send(CACHE, step, target, cache_buf)
+    cache_order = list(range(1, seq_count)) + [0]
+    for first in range(0, seq_count, together):
+        group = cache_order[first : first + together]
+        for step, (gathered, stats) in zip(group, cache_blocks([peers[step] for step in group])):
+            target = cache_src.at[peers[step]] if step else cache_buf.at[me]
+            target[:, :cols] = gathered
+            target[:, cols:] = stats
+            if step:
+                send(CACHE, step, target, cache_buf)
 
     own_query = unpack_query(me)
     pad = jnp.zeros((120, cols), jnp.float32)

time: 67.3 us -> 69.9 us (1.039)
  Pallas kernels: 63.6 us -> 66.2 us
    pallas_call x1, Pallas kernels: 63.6 us -> 66.2 us  [fused_device(): pl.pallas_call(functools.partial(layer_kernel, seq_count, head_count), ou...]
where the time goes in v3:
time: 69.9 us; the launch traced here: 69.6 us
  Pallas kernels  66.2 us (95%)
  local copies, waits for them, and re-layouts  2.75 us (4%)
    pallas_call x1, Pallas kernels, fused_device(): pl.pallas_call(functools.partial(layer_kernel, seq_count, head_count), ou...  66.2 us
    unnamed x2, local copies, waits for them, and re-layouts  2.75 us

profile of v3, /device:TPU:0, one launch (start us, length us, event | category | flops | bytes accessed | tf_op | source)
XLA Modules:
  0.0 69.6 jit_solution(7947381620893714252)
XLA Ops:
  0.6 66.2 %shard_map.104 = (bf16[4,16,256]{2,1,0:T(8,128)(2,1)}, bf16[4,16,256]{2,1,0:T(8,128)(2,1)}) custom-call(s32[16]{0:T(128)} %lengths_ref.1, bf16[4,16,256]{2,1,0:T(8,128)(2,1)} %tokens_ref.1, f32[1,128]{1,0:T(1,128)} %constant.2.clone.freq_ref, bf16[3,256,512]{2,1,0:T(8,128)(2,1)} %win_any.1, bf16[512,256]{1,0:T(8,128)(2,1)} %wout_hbm.1, ...), custom_call_target="tpu_custom_call" | custom-call | flops 184549376 | bytes 20971520 | tf_op jit(solution)/shard_map/pallas_call | solution.py:677
  66.8 1.4 %copy.13 = bf16[4,16,256]{2,1,0:T(8,128)(2,1)} copy(bf16[4,16,256]{2,1,0:T(8,128)(2,1)} %get-tuple-element.4) | data formatting | bytes 65536
  68.2 1.4 %copy.14 = bf16[4,16,256]{2,1,0:T(8,128)(2,1)} copy(bf16[4,16,256]{2,1,0:T(8,128)(2,1)} %get-tuple-element.5) | data formatting | bytes 65536
